TPU v7x, 256 devices: a whole 4x4x8 slice. The times are simulated.
256 devices in a mesh: group: 2 (over z_hi), dp: 8 (over x, core), tensor: 16 (over z_lo, y).
Axes of the slice: x: 4, y: 4, z: 8 (z_hi: 2, z_lo: 4; z = z_hi * 4 + z_lo), core: 2. Of those that a mesh axis runs over, the one named last changes fastest.
Arguments:
- teacher_hidden: bfloat16 [4096, 8192], P(('group', 'dp'), 'tensor'), may hold values from -6 to 6
- teacher_gain: float32 [8192], P('tensor'), may hold values from 0.1 to 1.9
- project_weight: bfloat16 [8192, 3584], P('tensor'), may hold values from -0.0625 to 0.0625
- student_hidden: bfloat16 [4096, 3584], P(('group', 'dp', 'tensor')), may hold values from -6 to 6
- student_gain: float32 [3584], replicated, may hold values from 0.1 to 1.9
- gate_weight: bfloat16 [3584, 9472], P(('group', 'dp'), 'tensor'), may hold values from -0.09375 to 0.09375
- up_weight: bfloat16 [3584, 9472], P(('group', 'dp'), 'tensor'), may hold values from -0.09375 to 0.09375
- down_weight: bfloat16 [9472, 3584], P('tensor', ('group', 'dp')), may hold values from -0.0625 to 0.0625
- owner_map: int32 [256, 1], P(('group', 'dp')), may hold values from 0 to 15; in each aligned block of 16 rows (0 to 15, 16 to 31, ...) at most 2 rows name the same one
- token_ids: int32 [4096], P(('group', 'dp', 'tensor')), may hold values from 0 to 511
- token_counts: int32 [256], P(('group', 'dp')), may hold values from 1 to 16
- id_weight: float32 [512], replicated, may hold values from 0.25 to 4
Outputs:
- student_out: bfloat16 [16, 16, 32, 3584], P(('group', 'dp'), 'tensor')
- down_grad: float32 [3584, 9472], P(('group', 'dp'), 'tensor')
Inputs may be any that keep to these rules, and one draw needn't show every extreme that they name: `owner_map`: of the 16 episodes of one index of group and dp (aligned blocks of 16 rows), at most 2 have the same owner; owner o is index o of group and dp in mesh order.
All inputs are finite; a program needn't handle non-finite values.
Results may differ from a plain program's by a relative error of at most 0.02.
Values may be sent and summed in bfloat16 or wider, within the bound.
No kernel may reach another device: no remote copies, remote signals or barrier semaphores. Data moves between devices by JAX's collectives and lax.ppermute only.
A program may use at most 128 MiB of HBM per device.

v0:
```python
import math

import jax
import jax.numpy as jnp
from jax import lax
from jax.experimental import pallas as pl
from jax.experimental.pallas import tpu as pltpu
from jax.sharding import Mesh
from jax.sharding import PartitionSpec as P

DT = 8192
EP_LEN = 16
AXES = {"group": 2, "x": 4, "core": 2, "z": 4, "y": 4}
OWNERS = ("group", "x", "core")
TENSOR = ("z", "y")
EPSILON = 1e-06
F32 = jnp.float32
BF16 = jnp.bfloat16


def shift(array, axis, by):
    size = AXES[axis]
    return lax.ppermute(array, axis, [(i, (i + by) % size) for i in range(size)])


def rolled(array, axis, name):
    doubled = jnp.concatenate([array, array], axis=axis)
    return lax.dynamic_slice_in_dim(doubled, lax.axis_index(name), array.shape[axis], axis)


def unrolled(array, axis, name):
    size = array.shape[axis]
    doubled = jnp.concatenate([array, array], axis=axis)
    return lax.dynamic_slice_in_dim(doubled, size - lax.axis_index(name), size, axis)


def exchange(array, axis, bits):
    return lax.ppermute(array, axis, [(i, i ^ bits) for i in range(AXES[axis])])


def relative_columns(rows):
    n = rows.shape[0]
    blocks = rows.reshape(n, 2, 4, 2, -1).transpose(1, 3, 2, 0, 4)
    blocks = rolled(rolled(rolled(blocks, 0, "group"), 1, "core"), 2, "x")
    return blocks.transpose(3, 0, 1, 2, 4).reshape(n, -1)


def absolute_columns(rows):
    n = rows.shape[0]
    blocks = rows.reshape(n, 2, 2, 4, -1).transpose(1, 2, 3, 0, 4)
    blocks = unrolled(unrolled(unrolled(blocks, 0, "group"), 1, "core"), 2, "x")
    return blocks.transpose(3, 0, 2, 1, 4).reshape(n, -1)


def after(array, *earlier):
    return lax.optimization_barrier((array, *earlier))[0]


def ring_pieces(piece, axis, *gates):
    half = (piece.shape[0] + 31) // 32 * 16
    behind = shift(piece, axis, 1)
    ahead = shift(piece, axis, -1)
    top = shift(after(behind[:half], *gates), axis, 1)
    bottom = shift(after(ahead[half:], *gates), axis, -1)
    return [piece, ahead, top, bottom, behind]


def swapped(pieces):
    return [shift(p, "core", 1) for p in pieces]


def ring_starts(pieces, block, low):
    return [low, low + block, low + 2 * block, low + 2 * block + pieces[2].shape[0], low + 3 * block]


def joined_product(rows, pieces, starts, skip):
    tokens, width, columns = rows.shape[0], sum(p.shape[0] for p in pieces), pieces[0].shape[1]
    count = len(pieces)

    def kernel(rows_ref, *refs):
        out_ref, whole, sems = refs[count:]
        copies = [
            pltpu.make_async_copy(refs[k], whole.at[pl.ds(starts[k], pieces[k].shape[0]), :], sems.at[k])
            for k in range(count)
        ]
        for c in copies:
            c.start()
        total = None
        for core in range(2):
            for c in copies[core * count // 2 : (core + 1) * count // 2]:
                c.wait()
            span = slice(core * width // 2, (core + 1) * width // 2)
            part = jnp.dot(rows_ref[:, span], whole[span, :], preferred_element_type=F32)
            total = part if total is None else total + part
        out_ref[...] = total[:, skip:]

    out = jax.ShapeDtypeStruct((tokens, columns - skip), F32)
    return pl.pallas_call(
        kernel,
        grid=(1,),
        in_specs=[
            pl.BlockSpec((tokens, width), lambda i: (0, 0)),
            *(pl.BlockSpec(memory_space=pltpu.HBM) for _ in pieces),
        ],
        out_specs=pl.BlockSpec(out.shape, lambda i: (0, 0)),
        out_shape=out,
        scratch_shapes=[pltpu.VMEM((width, columns), BF16), pltpu.SemaphoreType.DMA((count,))],
        compiler_params=pltpu.CompilerParams(vmem_limit_bytes=58 * 2**20),
    )(rows, *pieces)


def feed_forward(rows, near_sums, far, far_starts, near, near_starts, hidden):
    tokens, columns = rows.shape[0], far[0].shape[1]
    width = sum(p.shape[0] for p in far)
    lanes = -(-hidden // 128) * 128
    share = tokens // 4

    def kernel(rows_ref, near_sums_ref, *refs):
        far_refs, near_refs = refs[: len(far)], refs[len(far) : len(far) + len(near)]
        rest = refs[len(far) + len(near) :]
        activated_ref, far_outs, near_outs = rest[0], rest[1:5], rest[5:9]
        whole, near_down, padded, far_sems, near_sems = rest[9:]
        far_copies = [
            pltpu.make_async_copy(ref, whole.at[pl.ds(low, ref.shape[0]), :], far_sems.at[k])
            for k, (ref, low) in enumerate(zip(far_refs, far_starts))
        ]
        near_copies = [
            pltpu.make_async_copy(
                ref.at[:, pl.ds(0, lanes)], near_down.at[pl.ds(low, ref.shape[0]), :], near_sems.at[k]
            )
            for k, (ref, low) in enumerate(zip(near_refs, near_starts))
        ]
        for c in far_copies + near_copies:
            c.start()
        padded[...] = jnp.zeros_like(padded)
        total = near_sums_ref[...]
        for core in range(2):
            for c in far_copies[core * len(far) // 2 : (core + 1) * len(far) // 2]:
                c.wait()
            span = slice(core * width // 2, (core + 1) * width // 2)
            part = jnp.dot(rows_ref[:, span], whole[span, :], preferred_element_type=F32)
            total = total + part[:, hidden:]
        gate, up = total[:, :hidden], total[:, hidden:]
        activated = (gate / (1.0 + jnp.exp(-gate)) * up).astype(BF16)
        activated_ref[...] = activated
        padded[:, :hidden] = activated
        for c in near_copies:
            c.wait()
        for down, outs in ((whole[:, :lanes], far_outs), (near_down[...], near_outs)):
            branch = lax.dot_general(
                padded[...], down, (((1,), (1,)), ((), ())), preferred_element_type=F32
            ).astype(BF16)
            for k, out in enumerate(outs):
                out[...] = branch[k * share : (k + 1) * share]

    block = jax.ShapeDtypeStruct((share, width), BF16)
    outs = [jax.ShapeDtypeStruct((tokens, hidden), BF16), *[block] * 8]
    activated, *blocks = pl.pallas_call(
        kernel,
        grid=(1,),
        in_specs=[
            pl.BlockSpec((tokens, width), lambda i: (0, 1)),
            pl.BlockSpec(near_sums.shape, lambda i: (0, 0)),
            *(pl.BlockSpec(memory_space=pltpu.HBM) for _ in far + near),
        ],
        out_specs=[pl.BlockSpec(o.shape, lambda i: (0, 0)) for o in outs],
        out_shape=outs,
        scratch_shapes=[
            pltpu.VMEM((width, columns), BF16),
            pltpu.VMEM((width, lanes), BF16),
            pltpu.VMEM((tokens, lanes), BF16),
            pltpu.SemaphoreType.DMA((len(far),)),
            pltpu.SemaphoreType.DMA((len(near),)),
        ],
        compiler_params=pltpu.CompilerParams(vmem_limit_bytes=58 * 2**20),
    )(rows, near_sums, *far, *near)
    return activated, blocks[:4], blocks[4:]


def teacher_parts(rows, gain, weight, positions):
    each = rows.shape[0] // EP_LEN
    share = rows.shape[0] // 4
    sizes = (share, share, share // 2, share // 2, share)

    def kernel(positions_ref, rows_ref, gain_ref, weight_ref, *rest):
        outs, scaled = rest[:-1], rest[-1]
        for k in range(EP_LEN):
            low = pl.multiple_of(positions_ref[k] * each, each)
            wide = rows_ref[pl.ds(low, each), :].astype(F32)
            scaled[k * each : (k + 1) * each, :] = (wide * gain_ref[...]).astype(BF16)
        product = jnp.dot(scaled[...], weight_ref[...], preferred_element_type=F32).astype(BF16)
        low = 0
        for out, size in zip(outs, sizes):
            out[...] = product[low : low + size]
            low += size

    return pl.pallas_call(
        kernel,
        in_specs=[
            pl.BlockSpec(memory_space=pltpu.SMEM),
            *(pl.BlockSpec(memory_space=pltpu.VMEM) for _ in range(3)),
        ],
        out_specs=[pl.BlockSpec(memory_space=pltpu.VMEM) for _ in sizes],
        out_shape=[jax.ShapeDtypeStruct((size, weight.shape[1]), BF16) for size in sizes],
        scratch_shapes=[pltpu.VMEM(rows.shape, BF16)],
        compiler_params=pltpu.CompilerParams(vmem_limit_bytes=40 * 2**20),
    )(positions, rows, gain[None, :], weight)


def gather_z(rows):
    return jnp.concatenate([rows, *(exchange(rows, "z", k) for k in (1, 2, 3))], axis=0)


def gather_z_doubling(rows):
    pair = jnp.concatenate([rows, exchange(rows, "z", 1)], axis=0)
    return jnp.concatenate([pair, exchange(pair, "z", 2)], axis=0)


def added(parts, arrived):
    total = parts.astype(F32)
    for a in arrived:
        total = total + a.astype(F32)
    return total


def scatter_y(blocks):
    return added(blocks[0], [shift(blocks[k], "y", k) for k in (1, 2, 3)])


def scatter_z(parts):
    n = parts.shape[0] // 4
    return added(parts[:n], [exchange(parts[k * n : (k + 1) * n], "z", k) for k in (1, 2, 3)])


def scatter_z_halving(parts, *gates):
    n = parts.shape[0] // 4
    pair = added(parts[: 2 * n], [exchange(parts[2 * n :], "z", 2)])
    return added(pair[:n], [exchange(after(pair[n:].astype(BF16), *gates), "z", 1)])


def scatter_ring(own, first, top, bottom, third, axis, *gates):
    half = top.shape[0]
    top, bottom = shift(top, axis, 1), shift(bottom, axis, -1)
    up = jnp.concatenate([first[:half] + top, first[half:]], axis=0)
    down = jnp.concatenate([third[:half], third[half:] + bottom], axis=0)
    up, down = after(up, *gates), after(down, *gates)
    return added(own, [shift(up, axis, 1), shift(down, axis, -1)])


def two_parts(values):
    high = lax.reduce_precision(values, 8, 7)
    both = jnp.concatenate([high, values - high], axis=1).astype(BF16)
    return jnp.pad(both, ((0, 0), (0, 128 - both.shape[1])))


def pick(onehot, rows):
    return jnp.dot(onehot.astype(BF16), rows, preferred_element_type=F32).astype(BF16)


def to_owners(rows, owner_local, gate):
    owner = owner_local[:, 0]
    index = jnp.arange(owner.shape[0], dtype=jnp.int32)
    earlier = (owner[None, :] == owner[:, None]) & (index[None, :] < index[:, None])
    rank = jnp.sum(earlier.astype(jnp.int32), axis=1)
    g, x, c = (lax.axis_index(a) for a in OWNERS)
    to_c = (owner % 2 + c) % 2
    to_g = (owner // 8 + g) % 2
    to_x = (owner // 2 % 4 - x) % 4
    place = (to_g * 4 + to_x) * 2 + rank
    slots = jnp.arange(16, dtype=jnp.int32)[:, None]
    stay = pick((slots == place[None, :]) & (to_c[None, :] == 0), rows)
    leave = pick((slots == place[None, :]) & (to_c[None, :] == 1), rows)
    arrived = shift(leave, "core", 1)
    kept = jnp.concatenate([stay[:8], arrived[:8]], axis=0)
    sent = after(jnp.concatenate([stay[8:], arrived[8:]], axis=0), gate)
    both = jnp.concatenate([kept, shift(sent, "group", 1)], axis=0)
    place = jnp.arange(32, dtype=jnp.int32)
    by_x = pick((place // 2 % 4 * 4 + place // 8) * 2 + place % 2 == place[:, None], both)
    groups = [by_x[8 * k : 8 * (k + 1)] for k in range(4)]
    here = jnp.concatenate([groups[0], *(shift(groups[k], "x", k) for k in (1, 2, 3))], axis=0)
    source = jnp.arange(32, dtype=jnp.int32)
    k, sg, sc, r = source // 8, source // 4 % 2, source // 2 % 2, source % 2
    final = (((g + sg) % 2 * 4 + (x - k) % 4) * 2 + (c + sc) % 2) * 2 + r
    return pick(jnp.arange(32, dtype=jnp.int32)[:, None] == final[None, :], here)


def local(
    teacher_hidden,
    teacher_gain,
    project_weight,
    student_hidden,
    student_gain,
    gate_weight,
    up_weight,
    down_weight,
    owner_map,
    token_ids,
    token_counts,
    id_weight,
):
    episodes = token_counts.shape[0]
    hidden = gate_weight.shape[1]
    width = student_hidden.shape[1]
    block = width // 4
    position = lax.axis_index(TENSOR)
    tokens_all = EP_LEN * episodes * lax.axis_size(OWNERS)

    near = jnp.concatenate([down_weight.T, gate_weight, up_weight], axis=1)
    rows_each = near.shape[0]
    near_far = shift(near, "group", 1)
    near_own = ring_pieces(near, "x")
    near_first, near_last = (near_own[1], near_own[4]), (near_own[2], near_own[3])
    near_other = swapped(near_own)
    far_own = ring_pieces(after(near_far, *near_other), "x")
    far_first = (far_own[1], far_own[4])
    far_other = swapped(far_own)

    student_hidden, teacher_hidden = after(student_hidden, near), after(teacher_hidden, near)
    wide = student_hidden.astype(F32)
    rescale = lax.rsqrt(jnp.mean(wide * wide, axis=1, keepdims=True) + EPSILON)
    normed = (wide * rescale * student_gain[None, :]).astype(BF16)
    both_rows = relative_columns(jnp.concatenate([normed, student_hidden], axis=0))
    student = both_rows[episodes:].astype(F32)
    widened = teacher_hidden.astype(F32)
    squares = jnp.sum(widened * widened, axis=1).reshape(EP_LEN, episodes).T
    column = jnp.concatenate([both_rows[:episodes], two_parts(squares)], axis=1)
    column = gather_z_doubling(after(column, near_far, *near_other))
    gathered_pieces = ring_pieces(after(column, *far_first, far_other[0]), "y", far_other[1], far_other[4])
    gathered = jnp.concatenate(gathered_pieces, axis=0)
    totals = jnp.sum(gathered[:, width:].reshape(EP_LEN, episodes, -1).astype(F32), axis=0)
    totals = totals[:, :EP_LEN] + totals[:, EP_LEN : 2 * EP_LEN]
    totals = jnp.sum(jnp.where(jnp.arange(EP_LEN)[None, :] == position, totals, 0.0), axis=1)
    inverse = lax.rsqrt(totals / DT + EPSILON)

    ahead = jnp.arange(EP_LEN, dtype=jnp.int32)
    positions = (lax.axis_index("z") ^ ahead % 4) * 4 + (lax.axis_index("y") + ahead // 4) % 4
    parts = teacher_parts(after(teacher_hidden, *near_last), teacher_gain, project_weight, positions)
    parts = [after(p, near_far, *near_other) for p in parts]
    total = scatter_ring(*parts, "y")
    total = scatter_z_halving(after(total.astype(BF16), far_own[2], far_own[3]))
    projected = (total * inverse[:, None]).astype(BF16)
    projected = relative_columns(projected).astype(F32)

    ids = jnp.arange(id_weight.shape[0], dtype=jnp.int32)
    looked = jnp.sum(jnp.where(token_ids[:, None] == ids[None, :], id_weight[None, :], 0.0), axis=1)
    weight = jnp.where(position < token_counts, looked, 0.0).astype(BF16).astype(F32)
    scale = 1.0 / math.sqrt(tokens_all)

    def starts(pieces, low):
        return ring_starts(pieces, rows_each, low) + ring_starts(pieces, rows_each, low + block)

    near_pieces, near_starts = near_own + near_other, starts(near_own, 0)
    near_sums = joined_product(gathered, near_pieces, near_starts, hidden)
    activated, far_branch, near_branch = feed_forward(
        gathered,
        after(near_sums, total),
        far_own + far_other,
        starts(far_own, 0),
        near_pieces,
        near_starts,
        hidden,
    )

    def gradient_half(far, branch_rows):
        columns = slice(far * 2 * block, (far + 1) * 2 * block)
        predicted = student[:, columns] + scatter_z(branch_rows)
        difference = predicted - projected[:, columns]
        return predicted, gather_z((weight[:, None] * difference * scale).astype(BF16))

    def owners_half(grad):
        mine, other = (
            jnp.einsum(
                "rc,rh->ch", grad[:, a : a + block], activated, preferred_element_type=F32
            ).astype(BF16)
            for a in (0, block)
        )
        both = mine + shift(other, "core", 1)
        quarter = block // 4
        blocks = [both[k * quarter // 2 : (k + 1) * quarter // 2] for k in range(8)]
        return scatter_ring(
            both[:quarter], both[quarter : 2 * quarter], blocks[4], blocks[5], both[3 * quarter :], "x"
        )

    far_rows = scatter_y(far_branch).astype(BF16)
    near_rows = scatter_y(near_branch).astype(BF16)
    far_predicted, far_column = gradient_half(1, far_rows)
    near_predicted, near_column = gradient_half(0, near_rows)
    far_ring, near_ring = ring_pieces(far_column, "y"), ring_pieces(near_column, "y")
    far_grad, near_grad = jnp.concatenate(far_ring, axis=0), jnp.concatenate(near_ring, axis=0)
    far_reduced = owners_half(far_grad)
    near_reduced = owners_half(near_grad)
    down_grad = near_reduced + shift(far_reduced.astype(BF16), "group", 1).astype(F32)

    predicted = [near_predicted, far_predicted]
    rows = jnp.concatenate([p.astype(BF16) for p in predicted], axis=1)
    student_out = to_owners(absolute_columns(rows), owner_map, far_ring[1])
    return (student_out[None, None], down_grad)


def solution(mesh):
    split = Mesh(mesh.devices.reshape(*AXES.values()), tuple(AXES))
    placed = (
        P(OWNERS, TENSOR),
        P(TENSOR),
        P(TENSOR, None),
        P((*OWNERS, *TENSOR), None),
        P(),
        P(OWNERS, TENSOR),
        P(OWNERS, TENSOR),
        P(TENSOR, OWNERS),
        P(OWNERS, None),
        P((*OWNERS, *TENSOR)),
        P(OWNERS),
        P(),
    )
    return jax.shard_map(
        local,
        mesh=split,
        in_specs=placed,
        out_specs=(P(OWNERS, TENSOR, None, None), P(OWNERS, TENSOR)),
        check_vma=False,
    )
```

profile of v0, /device:TPU:32, one launch (start us, length us, event | category | flops | bytes accessed | tf_op | source)
XLA Modules:
  0.0 268.3 jit_solution(9718118803056252300)
XLA Ops:
  5.5 6.3 %collective-permute-start = (bf16[224,1776]{1,0:T(8,128)(2,1)S(1)}, bf16[224,1776]{1,0:T(8,128)(2,1)}, u32[]{:S(2)}, u32[]{:S(2)}) collective-permute-start(bf16[224,1776]{1,0:T(8,128)(2,1)S(1)} %concatenate.94.refs_0_.refs_10_), channel_id=1, source_target_pairs={{0,128},{128,0},{1,129},{129,1},{2,130},{130,2},{3,131},{131,3},{4... | collective-permute-start | bytes 2386952 | tf_op jit(solution)/shard_map/ppermute | solution.py:23
  35.4 6.3 %collective-permute-done.5.refs_2_.refs_12_ = bf16[112,1776]{1,0:T(8,128)(2,1)} collective-permute-done((bf16[112,1776]{1,0:T(8,128)(2,1)}, bf16[112,1776]{1,0:T(8,128)(2,1)}, u32[]{:S(2)}, u32[]{:S(2)}) %collective-permute-start.5) | collective-permute-done | bytes 397856 | tf_op jit(solution)/shard_map/ppermute | solution.py:23
  43.8 4.1 %collective-permute-done.refs_0_ = bf16[224,1776]{1,0:T(8,128)(2,1)} collective-permute-done((bf16[224,1776]{1,0:T(8,128)(2,1)S(1)}, bf16[224,1776]{1,0:T(8,128)(2,1)}, u32[]{:S(2)}, u32[]{:S(2)}) %collective-permute-start) | collective-permute-done | bytes 795680 | tf_op jit(solution)/shard_map/ppermute | solution.py:23
  61.5 5.1 %collective-permute-done.21 = bf16[32,3584]{1,0:T(8,128)(2,1)S(1)} collective-permute-done((bf16[32,3584]{1,0:T(8,128)(2,1)S(1)}, bf16[32,3584]{1,0:T(8,128)(2,1)S(1)}, u32[]{:S(2)}, u32[]{:S(2)}) %collective-permute-start.21) | collective-permute-done | bytes 229408 | tf_op jit(solution)/shard_map/ppermute | solution.py:23
  69.7 9.1 %collective-permute-done.11 = bf16[32,3712]{1,0:T(8,128)(2,1)S(1)} collective-permute-done((bf16[32,3712]{1,0:T(8,128)(2,1)S(1)}, bf16[32,3712]{1,0:T(8,128)(2,1)S(1)}, u32[]{:S(2)}, u32[]{:S(2)}) %collective-permute-start.11) | collective-permute-done | bytes 237600 | tf_op jit(solution)/shard_map/ppermute | solution.py:38
  82.5 9.7 %collective-permute-done.24 = bf16[64,3584]{1,0:T(8,128)(2,1)S(1)} collective-permute-done((bf16[64,3584]{1,0:T(8,128)(2,1)S(1)}, bf16[64,3584]{1,0:T(8,128)(2,1)S(1)}, u32[]{:S(2)}, u32[]{:S(2)}) %collective-permute-start.24) | collective-permute-done | bytes 458784 | tf_op jit(solution)/shard_map/ppermute | solution.py:23
  93.8 8.3 %collective-permute-done.26.refs_3_ = bf16[112,1776]{1,0:T(8,128)(2,1)} collective-permute-done((bf16[112,1776]{1,0:T(8,128)(2,1)S(1)}, bf16[112,1776]{1,0:T(8,128)(2,1)}, u32[]{:S(2)}, u32[]{:S(2)}) %collective-permute-start.26) | collective-permute-done | bytes 397856 | tf_op jit(solution)/shard_map/ppermute | solution.py:23
  102.1 3.5 %collective-permute-start.27 = (bf16[32,3584]{1,0:T(8,128)(2,1)S(1)}, bf16[32,3584]{1,0:T(8,128)(2,1)S(1)}, u32[]{:S(2)}, u32[]{:S(2)}) collective-permute-start(bf16[32,3584]{1,0:T(8,128)(2,1)S(1)} %slice.215), channel_id=1, source_target_pairs={{0,8},{4,12},{8,0},{12,4},{1,9},{5,13},{9,1},{13,5},{2,10},{6,14},... | collective-permute-start | bytes 688136 | tf_op jit(solution)/shard_map/ppermute | solution.py:38
  107.9 3.7 %collective-permute-done.27 = bf16[32,3584]{1,0:T(8,128)(2,1)S(1)} collective-permute-done((bf16[32,3584]{1,0:T(8,128)(2,1)S(1)}, bf16[32,3584]{1,0:T(8,128)(2,1)S(1)}, u32[]{:S(2)}, u32[]{:S(2)}) %collective-permute-start.27) | collective-permute-done | bytes 229408 | tf_op jit(solution)/shard_map/ppermute | solution.py:38
  111.7 12.2 %collective-permute-start.28 = (bf16[16,3584]{1,0:T(8,128)(2,1)S(1)}, bf16[16,3584]{1,0:T(8,128)(2,1)S(1)}, u32[]{:S(2)}, u32[]{:S(2)}) collective-permute-start(bf16[16,3584]{1,0:T(8,128)(2,1)S(1)} %slice.377), channel_id=1, source_target_pairs={{0,4},{4,0},{8,12},{12,8},{1,5},{5,1},{9,13},{13,9},{2,6},{6,2},{1... | collective-permute-start | bytes 344072 | tf_op jit(solution)/shard_map/ppermute | solution.py:38
  126.8 3.6 %collective-permute-done.20 = bf16[32,3712]{1,0:T(8,128)(2,1)S(1)} collective-permute-done((bf16[32,3712]{1,0:T(8,128)(2,1)S(1)}, bf16[32,3712]{1,0:T(8,128)(2,1)S(1)}, u32[]{:S(2)}, u32[]{:S(2)}) %collective-permute-start.20) | collective-permute-done | bytes 237600 | tf_op jit(solution)/shard_map/ppermute | solution.py:23
  131.8 6.7 %shard_map.131.near_sums_ref = f32[256,1184]{1,0:T(8,128)} custom-call(bf16[256,3712]{1,0:T(8,128)(2,1)} %copy-done.3, bf16[224,1776]{1,0:T(8,128)(2,1)} %copy-done.4, bf16[224,1776]{1,0:T(8,128)(2,1)} %copy-done.7, bf16[112,1776]{1,0:T(8,128)(2,1)} %collective-permute-done.5.refs_2_.refs_12_, bf16[112,1776]{1,0:T(8,128)(2,1)} %collective-permute-done.7.refs_3_.refs_13_, ...), custom_call_target="tpu_custom_call" | custom-call | tf_op jit(solution)/shard_map/pallas_call | solution.py:98
  138.6 8.9 %shard_map.133 = (bf16[256,592]{1,0:T(8,128)(2,1)}, bf16[64,1792]{1,0:T(8,128)(2,1)}, bf16[64,1792]{1,0:T(8,128)(2,1)}, bf16[64,1792]{1,0:T(8,128)(2,1)}, bf16[6...) custom-call(bf16[256,3712]{1,0:T(8,128)(2,1)} %copy-done.3, ...), custom_call_target="tpu_custom_call" | custom-call | tf_op jit(solution)/shard_map/pallas_call | solution.py:158
  149.4 3.3 %collective-permute-start.38 = (bf16[64,1792]{1,0:T(8,128)(2,1)}, bf16[64,1792]{1,0:T(8,128)(2,1)S(1)}, u32[]{:S(2)}, u32[]{:S(2)}) collective-permute-start(bf16[64,1792]{1,0:T(8,128)(2,1)} %get-tuple-element.58), channel_id=1, source_target_pairs={{0,2},{1,3},{2,0},{3,1},{4,6},{5,7},{6,4},{7,5},{8,10},{9,11},{10,... | collective-permute-start | bytes 688136 | tf_op jit(solution)/shard_map/ppermute | solution.py:23
  156.0 4.7 %collective-permute-done.37 = bf16[64,1792]{1,0:T(8,128)(2,1)S(1)} collective-permute-done((bf16[64,1792]{1,0:T(8,128)(2,1)}, bf16[64,1792]{1,0:T(8,128)(2,1)S(1)}, u32[]{:S(2)}, u32[]{:S(2)}) %collective-permute-start.37) | collective-permute-done | bytes 229408 | tf_op jit(solution)/shard_map/ppermute | solution.py:23
  160.7 3.8 %collective-permute-done.38 = bf16[64,1792]{1,0:T(8,128)(2,1)S(1)} collective-permute-done((bf16[64,1792]{1,0:T(8,128)(2,1)}, bf16[64,1792]{1,0:T(8,128)(2,1)S(1)}, u32[]{:S(2)}, u32[]{:S(2)}) %collective-permute-start.38) | collective-permute-done | bytes 229408 | tf_op jit(solution)/shard_map/ppermute | solution.py:23
  188.4 4.1 %collective-permute-start.55 = (bf16[64,1792]{1,0:T(8,128)(2,1)S(1)}, bf16[64,1792]{1,0:T(8,128)(2,1)S(1)}, u32[]{:S(2)}, u32[]{:S(2)}) collective-permute-start(bf16[64,1792]{1,0:T(8,128)(2,1)S(1)} %pad_maximum_fusion.10), channel_id=1, source_target_pairs={{0,3},{1,0},{2,1},{3,2},{4,7},{5,4},{6,5},{7,6},{8,11},{9,8},{10,9... | collective-permute-start | bytes 688136 | tf_op jit(solution)/shard_map/ppermute | solution.py:23
  192.5 3.5 %collective-permute-start.47 = (bf16[64,1792]{1,0:T(8,128)(2,1)S(1)}, bf16[64,1792]{1,0:T(8,128)(2,1)S(1)}, u32[]{:S(2)}, u32[]{:S(2)}) collective-permute-start(bf16[64,1792]{1,0:T(8,128)(2,1)S(1)} %pad_maximum_fusion.9), channel_id=1, source_target_pairs={{0,3},{1,0},{2,1},{3,2},{4,7},{5,4},{6,5},{7,6},{8,11},{9,8},{10,9... | collective-permute-start | bytes 688136 | tf_op jit(solution)/shard_map/ppermute | solution.py:23
  196.2 6.0 %collective-permute-done.56 = bf16[64,1792]{1,0:T(8,128)(2,1)S(1)} collective-permute-done((bf16[64,1792]{1,0:T(8,128)(2,1)S(1)}, bf16[64,1792]{1,0:T(8,128)(2,1)S(1)}, u32[]{:S(2)}, u32[]{:S(2)}) %collective-permute-start.56) | collective-permute-done | bytes 229408 | tf_op jit(solution)/shard_map/ppermute | solution.py:23
  210.5 5.7 %collective-permute-start.48 = (bf16[16,3584]{1,0:T(8,128)(2,1)S(1)}, bf16[16,3584]{1,0:T(8,128)(2,1)S(1)}, u32[]{:S(2)}, u32[]{:S(2)}) collective-permute-start(bf16[16,3584]{1,0:T(8,128)(2,1)S(1)} %pad_maximum_fusion.13), channel_id=1, source_target_pairs={{0,128},{128,0},{1,129},{129,1},{2,130},{130,2},{3,131},{131,3},{4... | collective-permute-start | bytes 344072 | tf_op jit(solution)/shard_map/ppermute | solution.py:23
  225.2 4.7 %collective-permute-done.68 = bf16[112,592]{0,1:T(8,128)(2,1)S(1)} collective-permute-done((bf16[112,592]{0,1:T(8,128)(2,1)S(1)}, bf16[112,592]{0,1:T(8,128)(2,1)S(1)}, u32[]{:S(2)}, u32[]{:S(2)}) %collective-permute-start.68) | collective-permute-done | bytes 132640 | tf_op jit(solution)/shard_map/ppermute | solution.py:23
  237.1 3.3 %collective-permute-start.71 = (bf16[224,592]{0,1:T(8,128)(2,1)S(1)}, bf16[224,592]{0,1:T(8,128)(2,1)S(1)}, u32[]{:S(2)}, u32[]{:S(2)}) collective-permute-start(bf16[224,592]{0,1:T(8,128)(2,1)S(1)} %pad_maximum_fusion.6), channel_id=1, source_target_pairs={{0,96},{32,0},{64,32},{96,64},{1,97},{33,1},{65,33},{97,65},{2,98}... | collective-permute-start | bytes 795656 | tf_op jit(solution)/shard_map/ppermute | solution.py:23
  243.1 6.3 %collective-permute-done.69 = bf16[224,592]{0,1:T(8,128)(2,1)S(1)} collective-permute-done((bf16[224,592]{0,1:T(8,128)(2,1)S(1)}, bf16[224,592]{0,1:T(8,128)(2,1)S(1)}, u32[]{:S(2)}, u32[]{:S(2)}) %collective-permute-start.69) | collective-permute-done | bytes 265248 | tf_op jit(solution)/shard_map/ppermute | solution.py:23
  258.3 8.7 %collective-permute-done.72 = bf16[224,592]{0,1:T(8,128)(2,1)S(1)} collective-permute-done((bf16[224,592]{0,1:T(8,128)(2,1)S(1)}, bf16[224,592]{0,1:T(8,128)(2,1)S(1)}, u32[]{:S(2)}, u32[]{:S(2)}) %collective-permute-start.72) | collective-permute-done | bytes 265248 | tf_op jit(solution)/shard_map/ppermute | solution.py:23
  (289 shorter events, 124.6 us)
Async XLA Ops:
  2.2 25.8 %collective-permute-start.4 = (bf16[224,1776]{1,0:T(8,128)(2,1)S(1)}, bf16[224,1776]{1,0:T(8,128)(2,1)S(1)}, u32[]{:S(2)}, u32[]{:S(2)}) collective-permute-start(bf16[224,1776]{1,0:T(8,128)(2,1)S(1)} %concatenate.94.refs_0_.refs_10_), channel_id=1, source_target_pairs={{0,32},{32,64},{64,96},{96,0},{1,33},{33,65},{65,97},{97,1},{2,34}... | collective-permute-start | bytes 2386952 | tf_op jit(solution)/shard_map/ppermute | solution.py:23
  3.8 25.3 %collective-permute-start.2 = (bf16[224,1776]{1,0:T(8,128)(2,1)S(1)}, bf16[224,1776]{1,0:T(8,128)(2,1)S(1)}, u32[]{:S(2)}, u32[]{:S(2)}) collective-permute-start(bf16[224,1776]{1,0:T(8,128)(2,1)S(1)} %concatenate.94.refs_0_.refs_10_), channel_id=1, source_target_pairs={{0,96},{32,0},{64,32},{96,64},{1,97},{33,1},{65,33},{97,65},{2,98}... | collective-permute-start | bytes 2386952 | tf_op jit(solution)/shard_map/ppermute | solution.py:23
  5.5 27.3 %collective-permute-start.1 = (bf16[224,1776]{1,0:T(8,128)(2,1)S(1)}, bf16[224,1776]{1,0:T(8,128)(2,1)S(1)}, u32[]{:S(2)}, u32[]{:S(2)}) collective-permute-start(bf16[224,1776]{1,0:T(8,128)(2,1)S(1)} %concatenate.94.refs_0_.refs_10_), channel_id=1, source_target_pairs={{0,16},{16,0},{1,17},{17,1},{2,18},{18,2},{3,19},{19,3},{4,20},{20... | collective-permute-start | bytes 2386952 | tf_op jit(solution)/shard_map/ppermute | solution.py:23
  5.5 42.3 %collective-permute-start = (bf16[224,1776]{1,0:T(8,128)(2,1)S(1)}, bf16[224,1776]{1,0:T(8,128)(2,1)}, u32[]{:S(2)}, u32[]{:S(2)}) collective-permute-start(bf16[224,1776]{1,0:T(8,128)(2,1)S(1)} %concatenate.94.refs_0_.refs_10_), channel_id=1, source_target_pairs={{0,128},{128,0},{1,129},{129,1},{2,130},{130,2},{3,131},{131,3},{4... | collective-permute-start | bytes 2386952 | tf_op jit(solution)/shard_map/ppermute | solution.py:23
  32.8 15.1 %collective-permute-start.3 = (bf16[224,1776]{1,0:T(8,128)(2,1)S(1)}, bf16[224,1776]{1,0:T(8,128)(2,1)}, u32[]{:S(2)}, u32[]{:S(2)}) collective-permute-start(bf16[224,1776]{1,0:T(8,128)(2,1)S(1)} %collective-permute-done.2.refs_1_.refs_11_), channel_id=1, source_target_pairs={{0,16},{16,0},{1,17},{17,1},{2,18},{18,2},{3,19},{19,3},{4,20},{20... | collective-permute-start | bytes 2386952 | tf_op jit(solution)/shard_map/ppermute | solution.py:23
  32.8 15.1 %collective-permute-start.9 = (bf16[224,1776]{1,0:T(8,128)(2,1)S(1)}, bf16[224,1776]{1,0:T(8,128)(2,1)}, u32[]{:S(2)}, u32[]{:S(2)}) collective-permute-start(bf16[224,1776]{1,0:T(8,128)(2,1)S(1)} %collective-permute-done.4.refs_4_.refs_14_), channel_id=1, source_target_pairs={{0,16},{16,0},{1,17},{17,1},{2,18},{18,2},{3,19},{19,3},{4,20},{20... | collective-permute-start | bytes 2386952 | tf_op jit(solution)/shard_map/ppermute | solution.py:23
  53.7 27.8 %collective-permute-start.13 = (bf16[224,1776]{1,0:T(8,128)(2,1)}, bf16[224,1776]{1,0:T(8,128)(2,1)S(1)}, u32[]{:S(2)}, u32[]{:S(2)}) collective-permute-start(bf16[224,1776]{1,0:T(8,128)(2,1)} %collective-permute-done.refs_0_), channel_id=1, source_target_pairs={{0,32},{32,64},{64,96},{96,0},{1,33},{33,65},{65,97},{97,1},{2,34}... | collective-permute-start | bytes 2386952 | tf_op jit(solution)/shard_map/ppermute | solution.py:23
  54.1 27.6 %collective-permute-start.12 = (bf16[224,1776]{1,0:T(8,128)(2,1)}, bf16[224,1776]{1,0:T(8,128)(2,1)S(1)}, u32[]{:S(2)}, u32[]{:S(2)}) collective-permute-start(bf16[224,1776]{1,0:T(8,128)(2,1)} %collective-permute-done.refs_0_), channel_id=1, source_target_pairs={{0,96},{32,0},{64,32},{96,64},{1,97},{33,1},{65,33},{97,65},{2,98}... | collective-permute-start | bytes 2386952 | tf_op jit(solution)/shard_map/ppermute | solution.py:23
  57.2 24.4 %collective-permute-start.14 = (bf16[224,1776]{1,0:T(8,128)(2,1)}, bf16[224,1776]{1,0:T(8,128)(2,1)S(1)}, u32[]{:S(2)}, u32[]{:S(2)}) collective-permute-start(bf16[224,1776]{1,0:T(8,128)(2,1)} %collective-permute-done.refs_0_), channel_id=1, source_target_pairs={{0,16},{16,0},{1,17},{17,1},{2,18},{18,2},{3,19},{19,3},{4,20},{20... | collective-permute-start | bytes 2386952 | tf_op jit(solution)/shard_map/ppermute | solution.py:23
  81.7 23.9 %collective-permute-start.15 = (bf16[64,3712]{1,0:T(8,128)(2,1)S(1)}, bf16[64,3712]{1,0:T(8,128)(2,1)S(1)}, u32[]{:S(2)}, u32[]{:S(2)}) collective-permute-start(bf16[64,3712]{1,0:T(8,128)(2,1)S(1)} %pad_maximum_fusion), channel_id=1, source_target_pairs={{0,3},{1,0},{2,1},{3,2},{4,7},{5,4},{6,5},{7,6},{8,11},{9,8},{10,9... | collective-permute-start | bytes 1425416 | tf_op jit(solution)/shard_map/ppermute | solution.py:23
  105.6 33.0 %collective-permute-start.29 = (bf16[112,1776]{1,0:T(8,128)(2,1)S(1)}, bf16[112,1776]{1,0:T(8,128)(2,1)}, u32[]{:S(2)}, u32[]{:S(2)}) collective-permute-start(bf16[112,1776]{1,0:T(8,128)(2,1)S(1)} %collective-permute-done.25.refs_2_), channel_id=1, source_target_pairs={{0,16},{16,0},{1,17},{17,1},{2,18},{18,2},{3,19},{19,3},{4,20},{20... | collective-permute-start | bytes 1193480 | tf_op jit(solution)/shard_map/ppermute | solution.py:23
  105.7 32.9 %collective-permute-start.30 = (bf16[112,1776]{1,0:T(8,128)(2,1)}, bf16[112,1776]{1,0:T(8,128)(2,1)}, u32[]{:S(2)}, u32[]{:S(2)}) collective-permute-start(bf16[112,1776]{1,0:T(8,128)(2,1)} %collective-permute-done.26.refs_3_), channel_id=1, source_target_pairs={{0,16},{16,0},{1,17},{17,1},{2,18},{18,2},{3,19},{19,3},{4,20},{20... | collective-permute-start | bytes 1193480 | tf_op jit(solution)/shard_map/ppermute | solution.py:23
  106.3 20.5 %collective-permute-start.19 = (bf16[32,3712]{1,0:T(8,128)(2,1)S(1)}, bf16[32,3712]{1,0:T(8,128)(2,1)S(1)}, u32[]{:S(2)}, u32[]{:S(2)}) collective-permute-start(bf16[32,3712]{1,0:T(8,128)(2,1)S(1)} %slice.267), channel_id=1, source_target_pairs={{0,1},{1,2},{2,3},{3,0},{4,5},{5,6},{6,7},{7,4},{8,9},{9,10},{10,1... | collective-permute-start | bytes 712712 | tf_op jit(solution)/shard_map/ppermute | solution.py:23
  111.7 19.1 %collective-permute-start.28 = (bf16[16,3584]{1,0:T(8,128)(2,1)S(1)}, bf16[16,3584]{1,0:T(8,128)(2,1)S(1)}, u32[]{:S(2)}, u32[]{:S(2)}) collective-permute-start(bf16[16,3584]{1,0:T(8,128)(2,1)S(1)} %slice.377), channel_id=1, source_target_pairs={{0,4},{4,0},{8,12},{12,8},{1,5},{5,1},{9,13},{13,9},{2,6},{6,2},{1... | collective-permute-start | bytes 344072 | tf_op jit(solution)/shard_map/ppermute | solution.py:38
  149.4 15.1 %collective-permute-start.38 = (bf16[64,1792]{1,0:T(8,128)(2,1)}, bf16[64,1792]{1,0:T(8,128)(2,1)S(1)}, u32[]{:S(2)}, u32[]{:S(2)}) collective-permute-start(bf16[64,1792]{1,0:T(8,128)(2,1)} %get-tuple-element.58), channel_id=1, source_target_pairs={{0,2},{1,3},{2,0},{3,1},{4,6},{5,7},{6,4},{7,5},{8,10},{9,11},{10,... | collective-permute-start | bytes 688136 | tf_op jit(solution)/shard_map/ppermute | solution.py:23
  153.8 14.2 %collective-permute-start.31 = (bf16[64,1792]{1,0:T(8,128)(2,1)}, bf16[64,1792]{1,0:T(8,128)(2,1)S(1)}, u32[]{:S(2)}, u32[]{:S(2)}) collective-permute-start(bf16[64,1792]{1,0:T(8,128)(2,1)} %get-tuple-element.53), channel_id=1, source_target_pairs={{0,1},{1,2},{2,3},{3,0},{4,5},{5,6},{6,7},{7,4},{8,9},{9,10},{10,1... | collective-permute-start | bytes 688136 | tf_op jit(solution)/shard_map/ppermute | solution.py:23
  154.8 15.8 %collective-permute-start.32 = (bf16[64,1792]{1,0:T(8,128)(2,1)}, bf16[64,1792]{1,0:T(8,128)(2,1)S(1)}, u32[]{:S(2)}, u32[]{:S(2)}) collective-permute-start(bf16[64,1792]{1,0:T(8,128)(2,1)} %get-tuple-element.54), channel_id=1, source_target_pairs={{0,2},{1,3},{2,0},{3,1},{4,6},{5,7},{6,4},{7,5},{8,10},{9,11},{10,... | collective-permute-start | bytes 688136 | tf_op jit(solution)/shard_map/ppermute | solution.py:23
  188.4 14.1 %collective-permute-start.55 = (bf16[64,1792]{1,0:T(8,128)(2,1)S(1)}, bf16[64,1792]{1,0:T(8,128)(2,1)S(1)}, u32[]{:S(2)}, u32[]{:S(2)}) collective-permute-start(bf16[64,1792]{1,0:T(8,128)(2,1)S(1)} %pad_maximum_fusion.10), channel_id=1, source_target_pairs={{0,3},{1,0},{2,1},{3,2},{4,7},{5,4},{6,5},{7,6},{8,11},{9,8},{10,9... | collective-permute-start | bytes 688136 | tf_op jit(solution)/shard_map/ppermute | solution.py:23
  192.5 14.6 %collective-permute-start.47 = (bf16[64,1792]{1,0:T(8,128)(2,1)S(1)}, bf16[64,1792]{1,0:T(8,128)(2,1)S(1)}, u32[]{:S(2)}, u32[]{:S(2)}) collective-permute-start(bf16[64,1792]{1,0:T(8,128)(2,1)S(1)} %pad_maximum_fusion.9), channel_id=1, source_target_pairs={{0,3},{1,0},{2,1},{3,2},{4,7},{5,4},{6,5},{7,6},{8,11},{9,8},{10,9... | collective-permute-start | bytes 688136 | tf_op jit(solution)/shard_map/ppermute | solution.py:23
  202.2 14.1 %collective-permute-start.57 = (bf16[32,1792]{1,0:T(8,128)(2,1)S(1)}, bf16[32,1792]{1,0:T(8,128)(2,1)S(1)}, u32[]{:S(2)}, u32[]{:S(2)}) collective-permute-start(bf16[32,1792]{1,0:T(8,128)(2,1)S(1)} %slice.295), channel_id=1, source_target_pairs={{0,1},{1,2},{2,3},{3,0},{4,5},{5,6},{6,7},{7,4},{8,9},{9,10},{10,1... | collective-permute-start | bytes 344072 | tf_op jit(solution)/shard_map/ppermute | solution.py:23
  220.6 31.4 %collective-permute-start.49 = (bf16[8,3584]{1,0:T(8,128)(2,1)S(1)}, bf16[8,3584]{1,0:T(8,128)(2,1)S(1)}, u32[]{:S(2)}, u32[]{:S(2)}) collective-permute-start(bf16[8,3584]{1,0:T(8,128)(2,1)S(1)} %get-tuple-element.95), channel_id=1, source_target_pairs={{0,32},{32,64},{64,96},{96,0},{1,33},{33,65},{65,97},{97,1},{2,34}... | collective-permute-start | bytes 172040 | tf_op jit(solution)/shard_map/ppermute | solution.py:23
  233.0 25.2 %collective-permute-start.61 = (bf16[224,592]{0,1:T(8,128)(2,1)S(1)}, bf16[224,592]{0,1:T(8,128)(2,1)S(1)}, u32[]{:S(2)}, u32[]{:S(2)}) collective-permute-start(bf16[224,592]{0,1:T(8,128)(2,1)S(1)} %pad_maximum_fusion.3), channel_id=1, source_target_pairs={{0,32},{32,64},{64,96},{96,0},{1,33},{33,65},{65,97},{97,1},{2,34}... | collective-permute-start | bytes 795656 | tf_op jit(solution)/shard_map/ppermute | solution.py:23
  240.6 17.6 %collective-permute-start.63 = (bf16[224,592]{0,1:T(8,128)(2,1)S(1)}, bf16[224,592]{0,1:T(8,128)(2,1)S(1)}, u32[]{:S(2)}, u32[]{:S(2)}) collective-permute-start(bf16[224,592]{0,1:T(8,128)(2,1)S(1)} %pad_maximum_fusion.4), channel_id=1, source_target_pairs={{0,96},{32,0},{64,32},{96,64},{1,97},{33,1},{65,33},{97,65},{2,98}... | collective-permute-start | bytes 795656 | tf_op jit(solution)/shard_map/ppermute | solution.py:23
  249.5 17.4 %collective-permute-start.72 = (bf16[224,592]{0,1:T(8,128)(2,1)S(1)}, bf16[224,592]{0,1:T(8,128)(2,1)S(1)}, u32[]{:S(2)}, u32[]{:S(2)}) collective-permute-start(bf16[224,592]{0,1:T(8,128)(2,1)S(1)} %add_convert_fusion.1), channel_id=1, source_target_pairs={{0,128},{128,0},{1,129},{129,1},{2,130},{130,2},{3,131},{131,3},{4... | collective-permute-start | bytes 795656 | tf_op jit(solution)/shard_map/ppermute | solution.py:23
  (72 other events, 772.4 us)
where the time goes:
time: 273 us; the launch traced here: 268 us
  starting transfers between devices  110 us (40%)
  waiting for transfers between devices  97.2 us (36%)
  other arithmetic  21.6 us (8%)
  Pallas kernels  17.3 us (6%)
  local copies, waits for them, and re-layouts  16.7 us (6%)
  matrix products  3.58 us (1%)
    ppermute x57, waiting for transfers between devices, shift(): lax.ppermute(array, axis, [(i, (i + by) % size) for i in range(size)])  81.5 us
    ppermute x57, starting transfers between devices, shift(): lax.ppermute(array, axis, [(i, (i + by) % size) for i in range(size)])  75.9 us
    ppermute x16, starting transfers between devices, exchange(): return lax.ppermute(array, axis, [(i, i ^ bits) for i in range(AXES[axis])])  34.1 us
    ppermute x16, waiting for transfers between devices, exchange(): return lax.ppermute(array, axis, [(i, i ^ bits) for i in range(AXES[axis])])  15.7 us
    pallas_call x1, Pallas kernels, feed_forward(): pl.pallas_call(kernel, grid=(1,), in_specs=[pl.BlockSpec((tokens, width),...  8.93 us
    pallas_call x1, Pallas kernels, joined_product(): pl.pallas_call(kernel, grid=(1,), in_specs=[pl.BlockSpec((tokens, width),...  6.75 us
  transfers between devices with their start and end apart: 73, of which 27 were waited for; matrix products, arithmetic and copies ran while one was open for 13% of the time, Pallas kernels for 3%

commit v1 on v0

--- a/solution.py
+++ b/solution.py
@@ -73,107 +73,60 @@
     return [low, low + block, low + 2 * block, low + 2 * block + pieces[2].shape[0], low + 3 * block]
 
 
-def joined_product(rows, pieces, starts, skip):
-    tokens, width, columns = rows.shape[0], sum(p.shape[0] for p in pieces), pieces[0].shape[1]
-    count = len(pieces)
+def feed_forward(rows, pieces, starts, hidden):
+    tokens, columns = rows.shape[0], pieces[0].shape[1]
+    width = sum(p.shape[0] for p in pieces)
+    lanes = -(-hidden // 128) * 128
+    count, groups = len(pieces), 4
+    share = tokens // 4
 
     def kernel(rows_ref, *refs):
-        out_ref, whole, sems = refs[count:]
+        activated_ref, outs = refs[count], refs[count + 1 : count + 9]
+        whole, padded, sems = refs[count + 9 :]
         copies = [
-            pltpu.make_async_copy(refs[k], whole.at[pl.ds(starts[k], pieces[k].shape[0]), :], sems.at[k])
-            for k in range(count)
+            pltpu.make_async_copy(ref, whole.at[pl.ds(low, ref.shape[0]), :], sems.at[k])
+            for k, (ref, low) in enumerate(zip(refs[:count], starts))
         ]
         for c in copies:
             c.start()
+        padded[...] = jnp.zeros_like(padded)
         total = None
-        for core in range(2):
-            for c in copies[core * count // 2 : (core + 1) * count // 2]:
+        for group in range(groups):
+            for c in copies[group * count // groups : (group + 1) * count // groups]:
                 c.wait()
-            span = slice(core * width // 2, (core + 1) * width // 2)
+            span = slice(group * width // groups, (group + 1) * width // groups)
             part = jnp.dot(rows_ref[:, span], whole[span, :], preferred_element_type=F32)
             total = part if total is None else total + part
-        out_ref[...] = total[:, skip:]
-
-    out = jax.ShapeDtypeStruct((tokens, columns - skip), F32)
-    return pl.pallas_call(
-        kernel,
-        grid=(1,),
-        in_specs=[
-            pl.BlockSpec((tokens, width), lambda i: (0, 0)),
-            *(pl.BlockSpec(memory_space=pltpu.HBM) for _ in pieces),
-        ],
-        out_specs=pl.BlockSpec(out.shape, lambda i: (0, 0)),
-        out_shape=out,
-        scratch_shapes=[pltpu.VMEM((width, columns), BF16), pltpu.SemaphoreType.DMA((count,))],
-        compiler_params=pltpu.CompilerParams(vmem_limit_bytes=58 * 2**20),
-    )(rows, *pieces)
-
-
-def feed_forward(rows, near_sums, far, far_starts, near, near_starts, hidden):
-    tokens, columns = rows.shape[0], far[0].shape[1]
-    width = sum(p.shape[0] for p in far)
-    lanes = -(-hidden // 128) * 128
-    share = tokens // 4
-
-    def kernel(rows_ref, near_sums_ref, *refs):
-        far_refs, near_refs = refs[: len(far)], refs[len(far) : len(far) + len(near)]
-        rest = refs[len(far) + len(near) :]
-        activated_ref, far_outs, near_outs = rest[0], rest[1:5], rest[5:9]
-        whole, near_down, padded, far_sems, near_sems = rest[9:]
-        far_copies = [
-            pltpu.make_async_copy(ref, whole.at[pl.ds(low, ref.shape[0]), :], far_sems.at[k])
-            for k, (ref, low) in enumerate(zip(far_refs, far_starts))
-        ]
-        near_copies = [
-            pltpu.make_async_copy(
-                ref.at[:, pl.ds(0, lanes)], near_down.at[pl.ds(low, ref.shape[0]), :], near_sems.at[k]
-            )
-            for k, (ref, low) in enumerate(zip(near_refs, near_starts))
-        ]
-        for c in far_copies + near_copies:
-            c.start()
-        padded[...] = jnp.zeros_like(padded)
-        total = near_sums_ref[...]
-        for core in range(2):
-            for c in far_copies[core * len(far) // 2 : (core + 1) * len(far) // 2]:
-                c.wait()
-            span = slice(core * width // 2, (core + 1) * width // 2)
-            part = jnp.dot(rows_ref[:, span], whole[span, :], preferred_element_type=F32)
-            total = total + part[:, hidden:]
-        gate, up = total[:, :hidden], total[:, hidden:]
+        gate, up = total[:, hidden : 2 * hidden], total[:, 2 * hidden :]
         activated = (gate / (1.0 + jnp.exp(-gate)) * up).astype(BF16)
         activated_ref[...] = activated
         padded[:, :hidden] = activated
-        for c in near_copies:
-            c.wait()
-        for down, outs in ((whole[:, :lanes], far_outs), (near_down[...], near_outs)):
+        for k in range(2):
+            down = whole[k * width // 2 : (k + 1) * width // 2, :lanes]
             branch = lax.dot_general(
                 padded[...], down, (((1,), (1,)), ((), ())), preferred_element_type=F32
             ).astype(BF16)
-            for k, out in enumerate(outs):
-                out[...] = branch[k * share : (k + 1) * share]
-
-    block = jax.ShapeDtypeStruct((share, width), BF16)
-    outs = [jax.ShapeDtypeStruct((tokens, hidden), BF16), *[block] * 8]
+            for r in range(4):
+                outs[4 * k + r][...] = branch[r * share : (r + 1) * share]
+
+    block = jax.ShapeDtypeStruct((share, width // 2), BF16)
+    out_shapes = [jax.ShapeDtypeStruct((tokens, hidden), BF16), *[block] * 8]
     activated, *blocks = pl.pallas_call(
         kernel,
         grid=(1,),
         in_specs=[
-            pl.BlockSpec((tokens, width), lambda i: (0, 1)),
-            pl.BlockSpec(near_sums.shape, lambda i: (0, 0)),
-            *(pl.BlockSpec(memory_space=pltpu.HBM) for _ in far + near),
+            pl.BlockSpec(rows.shape, lambda i: (0, 0)),
+            *(pl.BlockSpec(memory_space=pltpu.HBM) for _ in pieces),
         ],
-        out_specs=[pl.BlockSpec(o.shape, lambda i: (0, 0)) for o in outs],
-        out_shape=outs,
+        out_specs=[pl.BlockSpec(o.shape, lambda i: (0, 0)) for o in out_shapes],
+        out_shape=out_shapes,
         scratch_shapes=[
             pltpu.VMEM((width, columns), BF16),
-            pltpu.VMEM((width, lanes), BF16),
             pltpu.VMEM((tokens, lanes), BF16),
-            pltpu.SemaphoreType.DMA((len(far),)),
-            pltpu.SemaphoreType.DMA((len(near),)),
+            pltpu.SemaphoreType.DMA((count,)),
         ],
         compiler_params=pltpu.CompilerParams(vmem_limit_bytes=58 * 2**20),
-    )(rows, near_sums, *far, *near)
+    )(rows, *pieces)
     return activated, blocks[:4], blocks[4:]
 
 
@@ -310,7 +263,13 @@
     near_far = shift(near, "group", 1)
     near_own = ring_pieces(near, "x")
     near_first, near_last = (near_own[1], near_own[4]), (near_own[2], near_own[3])
-    near_other = swapped(near_own)
+    ahead = jnp.arange(EP_LEN, dtype=jnp.int32)
+    positions = (lax.axis_index("z") ^ ahead % 4) * 4 + (lax.axis_index("y") + ahead // 4) % 4
+    near_across = shift(near, "core", 1)
+    rows = after(teacher_hidden, near_across, *near_first)
+    parts = teacher_parts(rows, teacher_gain, project_weight, positions)
+    near_relayed = [after(p, parts[0]) for p in near_last]
+    near_other = [near_across, *swapped([near_own[1], *near_relayed, near_own[4]])]
     far_own = ring_pieces(after(near_far, *near_other), "x")
     far_first = (far_own[1], far_own[4])
     far_other = swapped(far_own)
@@ -324,7 +283,7 @@
     widened = teacher_hidden.astype(F32)
     squares = jnp.sum(widened * widened, axis=1).reshape(EP_LEN, episodes).T
     column = jnp.concatenate([both_rows[:episodes], two_parts(squares)], axis=1)
-    column = gather_z_doubling(after(column, near_far, *near_other))
+    column = gather_z_doubling(after(column, far_other[0], *near_other))
     gathered_pieces = ring_pieces(after(column, *far_first, far_other[0]), "y", far_other[1], far_other[4])
     gathered = jnp.concatenate(gathered_pieces, axis=0)
     totals = jnp.sum(gathered[:, width:].reshape(EP_LEN, episodes, -1).astype(F32), axis=0)
@@ -332,10 +291,6 @@
     totals = jnp.sum(jnp.where(jnp.arange(EP_LEN)[None, :] == position, totals, 0.0), axis=1)
     inverse = lax.rsqrt(totals / DT + EPSILON)
 
-    ahead = jnp.arange(EP_LEN, dtype=jnp.int32)
-    positions = (lax.axis_index("z") ^ ahead % 4) * 4 + (lax.axis_index("y") + ahead // 4) % 4
-    parts = teacher_parts(after(teacher_hidden, *near_last), teacher_gain, project_weight, positions)
-    parts = [after(p, near_far, *near_other) for p in parts]
     total = scatter_ring(*parts, "y")
     total = scatter_z_halving(after(total.astype(BF16), far_own[2], far_own[3]))
     projected = (total * inverse[:, None]).astype(BF16)
@@ -349,15 +304,10 @@
     def starts(pieces, low):
         return ring_starts(pieces, rows_each, low) + ring_starts(pieces, rows_each, low + block)
 
-    near_pieces, near_starts = near_own + near_other, starts(near_own, 0)
-    near_sums = joined_product(gathered, near_pieces, near_starts, hidden)
-    activated, far_branch, near_branch = feed_forward(
-        gathered,
-        after(near_sums, total),
-        far_own + far_other,
-        starts(far_own, 0),
-        near_pieces,
-        near_starts,
+    activated, near_branch, far_branch = feed_forward(
+        after(gathered, total),
+        near_own + near_other + far_own + far_other,
+        starts(near_own, 0) + starts(far_own, 2 * block),
         hidden,
     )
 

time: 273 us -> 259 us (0.949)
  local copies, waits for them, and re-layouts: 16.7 us -> 8.97 us
  other arithmetic: 21.6 us -> 15.7 us
  waiting for transfers between devices: 97.2 us -> 103 us
  Pallas kernels: 17.3 us -> 12.9 us
  starting transfers between devices: 110 us -> 107 us
    ppermute x57, waiting for transfers between devices: 81.5 us -> 91.4 us  [shift(): lax.ppermute(array, axis, [(i, (i + by) % size) for i in range(size)])]
    ppermute x16, starting transfers between devices: 34.1 us -> 25 us  [exchange(): return lax.ppermute(array, axis, [(i, i ^ bits) for i in range(AXES[axis])])]
    ppermute x57, starting transfers between devices: 75.9 us -> 82.3 us  [shift(): lax.ppermute(array, axis, [(i, (i + by) % size) for i in range(size)])]
    pallas_call x2 -> x1, Pallas kernels: 15.7 us -> 11.3 us  [feed_forward(): pl.pallas_call(kernel, grid=(1,), in_specs=[pl.BlockSpec(rows.shape, lamb...]
    ppermute x16, waiting for transfers between devices: 15.7 us -> 11.8 us  [exchange(): return lax.ppermute(array, axis, [(i, i ^ bits) for i in range(AXES[axis])])]
    reshape x4, local copies, waits for them, and re-layouts: 4.11 us -> 0.79 us  [relative_columns(): blocks = rows.reshape(n, 2, 4, 2, -1).transpose(1, 3, 2, 0, 4)]
    concatenate x4, other arithmetic: 4.44 us -> 1.14 us  [rolled(): doubled = jnp.concatenate([array, array], axis=axis)]
  transfers between devices with their start and end apart: 73 -> 73, of which waited for: 27 -> 27; matrix products, arithmetic and copies ran while one was open for 13% -> 9% of each run, Pallas kernels for 3% -> 1%
where the time goes in v1:
time: 259 us; the launch traced here: 254 us
  starting transfers between devices  107 us (41%)
  waiting for transfers between devices  103 us (40%)
  other arithmetic  15.7 us (6%)
  Pallas kernels  12.9 us (5%)
  local copies, waits for them, and re-layouts  8.97 us (3%)
  matrix products  3.52 us (1%)
    ppermute x57, waiting for transfers between devices, shift(): lax.ppermute(array, axis, [(i, (i + by) % size) for i in range(size)])  91.4 us
    ppermute x57, starting transfers between devices, shift(): lax.ppermute(array, axis, [(i, (i + by) % size) for i in range(size)])  82.3 us
    ppermute x16, starting transfers between devices, exchange(): return lax.ppermute(array, axis, [(i, i ^ bits) for i in range(AXES[axis])])  25 us
    ppermute x16, waiting for transfers between devices, exchange(): return lax.ppermute(array, axis, [(i, i ^ bits) for i in range(AXES[axis])])  11.8 us
    pallas_call x1, Pallas kernels, feed_forward(): pl.pallas_call(kernel, grid=(1,), in_specs=[pl.BlockSpec(rows.shape, lamb...  11.3 us
  transfers between devices with their start and end apart: 73, of which 27 were waited for; matrix products, arithmetic and copies ran while one was open for 9% of the time, Pallas kernels for 1%

profile of v1, /device:TPU:32, one launch (start us, length us, event | category | flops | bytes accessed | tf_op | source)
XLA Modules:
  0.0 253.7 jit_solution(6344094737166706790)
XLA Ops:
  5.1 6.3 %collective-permute-start = (bf16[224,1776]{1,0:T(8,128)(2,1)S(1)}, bf16[224,1776]{1,0:T(8,128)(2,1)}, u32[]{:S(2)}, u32[]{:S(2)}) collective-permute-start(bf16[224,1776]{1,0:T(8,128)(2,1)S(1)} %concatenate.94.refs_0_), channel_id=1, source_target_pairs={{0,128},{128,0},{1,129},{129,1},{2,130},{130,2},{3,131},{131,3},{4... | collective-permute-start | bytes 2386952 | tf_op jit(solution)/shard_map/ppermute | solution.py:23
  18.0 4.9 %collective-permute-done.2.refs_1_ = bf16[224,1776]{1,0:T(8,128)(2,1)S(1)} collective-permute-done((bf16[224,1776]{1,0:T(8,128)(2,1)S(1)}, bf16[224,1776]{1,0:T(8,128)(2,1)S(1)}, u32[]{:S(2)}, u32[]{:S(2)}) %collective-permute-start.2) | collective-permute-done | bytes 795680 | tf_op jit(solution)/shard_map/ppermute | solution.py:23
  22.9 3.4 %collective-permute-done.4.refs_4_ = bf16[224,1776]{1,0:T(8,128)(2,1)S(1)} collective-permute-done((bf16[224,1776]{1,0:T(8,128)(2,1)S(1)}, bf16[224,1776]{1,0:T(8,128)(2,1)S(1)}, u32[]{:S(2)}, u32[]{:S(2)}) %collective-permute-start.4) | collective-permute-done | bytes 795680 | tf_op jit(solution)/shard_map/ppermute | solution.py:23
  32.1 3.3 %collective-permute-start.7 = (bf16[112,1776]{1,0:T(8,128)(2,1)S(1)}, bf16[112,1776]{1,0:T(8,128)(2,1)S(1)}, u32[]{:S(2)}, u32[]{:S(2)}) collective-permute-start(bf16[112,1776]{1,0:T(8,128)(2,1)S(1)} %slice.266), channel_id=1, source_target_pairs={{0,96},{32,0},{64,32},{96,64},{1,97},{33,1},{65,33},{97,65},{2,98}... | collective-permute-start | bytes 1193480 | tf_op jit(solution)/shard_map/ppermute | solution.py:23
  38.6 5.0 %collective-permute-done.5.refs_2_ = bf16[112,1776]{1,0:T(8,128)(2,1)S(1)} collective-permute-done((bf16[112,1776]{1,0:T(8,128)(2,1)S(1)}, bf16[112,1776]{1,0:T(8,128)(2,1)S(1)}, u32[]{:S(2)}, u32[]{:S(2)}) %collective-permute-start.5) | collective-permute-done | bytes 397856 | tf_op jit(solution)/shard_map/ppermute | solution.py:23
  62.7 3.5 %collective-permute-done.24 = bf16[64,3584]{1,0:T(8,128)(2,1)} collective-permute-done((bf16[64,3584]{1,0:T(8,128)(2,1)}, bf16[64,3584]{1,0:T(8,128)(2,1)}, u32[]{:S(2)}, u32[]{:S(2)}) %collective-permute-start.24) | collective-permute-done | bytes 458784 | tf_op jit(solution)/shard_map/ppermute | solution.py:23
  67.6 9.2 %collective-permute-done.14.refs_14_ = bf16[224,1776]{1,0:T(8,128)(2,1)S(1)} collective-permute-done((bf16[224,1776]{1,0:T(8,128)(2,1)}, bf16[224,1776]{1,0:T(8,128)(2,1)S(1)}, u32[]{:S(2)}, u32[]{:S(2)}) %collective-permute-start.14) | collective-permute-done | bytes 795680 | tf_op jit(solution)/shard_map/ppermute | solution.py:23
  77.0 3.3 %collective-permute-start.26 = (bf16[112,1776]{1,0:T(8,128)(2,1)S(1)}, bf16[112,1776]{1,0:T(8,128)(2,1)S(1)}, u32[]{:S(2)}, u32[]{:S(2)}) collective-permute-start(bf16[112,1776]{1,0:T(8,128)(2,1)S(1)} %slice.270), channel_id=1, source_target_pairs={{0,96},{32,0},{64,32},{96,64},{1,97},{33,1},{65,33},{97,65},{2,98}... | collective-permute-start | bytes 1193480 | tf_op jit(solution)/shard_map/ppermute | solution.py:23
  83.3 5.1 %collective-permute-done.25.refs_12_ = bf16[112,1776]{1,0:T(8,128)(2,1)S(1)} collective-permute-done((bf16[112,1776]{1,0:T(8,128)(2,1)S(1)}, bf16[112,1776]{1,0:T(8,128)(2,1)S(1)}, u32[]{:S(2)}, u32[]{:S(2)}) %collective-permute-start.25) | collective-permute-done | bytes 397856 | tf_op jit(solution)/shard_map/ppermute | solution.py:23
  90.7 7.5 %collective-permute-done.27 = bf16[32,3584]{1,0:T(8,128)(2,1)S(1)} collective-permute-done((bf16[32,3584]{1,0:T(8,128)(2,1)S(1)}, bf16[32,3584]{1,0:T(8,128)(2,1)S(1)}, u32[]{:S(2)}, u32[]{:S(2)}) %collective-permute-start.27) | collective-permute-done | bytes 229408 | tf_op jit(solution)/shard_map/ppermute | solution.py:38
  101.7 11.6 %collective-permute-start.20 = (bf16[32,3712]{1,0:T(8,128)(2,1)S(1)}, bf16[32,3712]{1,0:T(8,128)(2,1)S(1)}, u32[]{:S(2)}, u32[]{:S(2)}) collective-permute-start(bf16[32,3712]{1,0:T(8,128)(2,1)S(1)} %slice.268), channel_id=1, source_target_pairs={{0,3},{1,0},{2,1},{3,2},{4,7},{5,4},{6,5},{7,6},{8,11},{9,8},{10,9... | collective-permute-start | bytes 712712 | tf_op jit(solution)/shard_map/ppermute | solution.py:23
  113.4 8.3 %collective-permute-done.19 = bf16[32,3712]{1,0:T(8,128)(2,1)S(1)} collective-permute-done((bf16[32,3712]{1,0:T(8,128)(2,1)S(1)}, bf16[32,3712]{1,0:T(8,128)(2,1)S(1)}, u32[]{:S(2)}, u32[]{:S(2)}) %collective-permute-start.19) | collective-permute-done | bytes 237600 | tf_op jit(solution)/shard_map/ppermute | solution.py:23
  123.3 11.3 %shard_map.132 = (bf16[256,592]{1,0:T(8,128)(2,1)}, bf16[64,1792]{1,0:T(8,128)(2,1)}, bf16[64,1792]{1,0:T(8,128)(2,1)}, bf16[64,1792]{1,0:T(8,128)(2,1)}, bf16[6...) custom-call(bf16[256,3712]{1,0:T(8,128)(2,1)} %copy-done.5, ...), custom_call_target="tpu_custom_call" | custom-call | tf_op jit(solution)/shard_map/pallas_call | solution.py:114
  141.5 8.1 %collective-permute-done.37 = bf16[64,1792]{1,0:T(8,128)(2,1)S(1)} collective-permute-done((bf16[64,1792]{1,0:T(8,128)(2,1)}, bf16[64,1792]{1,0:T(8,128)(2,1)S(1)}, u32[]{:S(2)}, u32[]{:S(2)}) %collective-permute-start.37) | collective-permute-done | bytes 229408 | tf_op jit(solution)/shard_map/ppermute | solution.py:23
  165.9 3.3 %collective-permute-start.52 = (bf16[16,1792]{1,0:T(8,128)(2,1)S(1)}, bf16[16,1792]{1,0:T(8,128)(2,1)S(1)}, u32[]{:S(2)}, u32[]{:S(2)}) collective-permute-start(bf16[16,1792]{1,0:T(8,128)(2,1)S(1)} %get-tuple-element.63), channel_id=1, source_target_pairs={{0,4},{4,0},{8,12},{12,8},{1,5},{5,1},{9,13},{13,9},{2,6},{6,2},{1... | collective-permute-start | bytes 172040 | tf_op jit(solution)/shard_map/ppermute | solution.py:38
  183.0 5.3 %collective-permute-done.56 = bf16[64,1792]{1,0:T(8,128)(2,1)S(1)} collective-permute-done((bf16[64,1792]{1,0:T(8,128)(2,1)S(1)}, bf16[64,1792]{1,0:T(8,128)(2,1)S(1)}, u32[]{:S(2)}, u32[]{:S(2)}) %collective-permute-start.56) | collective-permute-done | bytes 229408 | tf_op jit(solution)/shard_map/ppermute | solution.py:23
  188.4 3.5 %collective-permute-start.58 = (bf16[32,1792]{1,0:T(8,128)(2,1)S(1)}, bf16[32,1792]{1,0:T(8,128)(2,1)S(1)}, u32[]{:S(2)}, u32[]{:S(2)}) collective-permute-start(bf16[32,1792]{1,0:T(8,128)(2,1)S(1)} %slice.296), channel_id=1, source_target_pairs={{0,3},{1,0},{2,1},{3,2},{4,7},{5,4},{6,5},{7,6},{8,11},{9,8},{10,9... | collective-permute-start | bytes 344072 | tf_op jit(solution)/shard_map/ppermute | solution.py:23
  193.3 3.3 %collective-permute-start.66 = (bf16[32,1792]{1,0:T(8,128)(2,1)S(1)}, bf16[32,1792]{1,0:T(8,128)(2,1)S(1)}, u32[]{:S(2)}, u32[]{:S(2)}) collective-permute-start(bf16[32,1792]{1,0:T(8,128)(2,1)S(1)} %slice.307), channel_id=1, source_target_pairs={{0,3},{1,0},{2,1},{3,2},{4,7},{5,4},{6,5},{7,6},{8,11},{9,8},{10,9... | collective-permute-start | bytes 344072 | tf_op jit(solution)/shard_map/ppermute | solution.py:23
  196.6 5.0 %collective-permute-start.48 = (bf16[16,3584]{1,0:T(8,128)(2,1)S(1)}, bf16[16,3584]{1,0:T(8,128)(2,1)S(1)}, u32[]{:S(2)}, u32[]{:S(2)}) collective-permute-start(bf16[16,3584]{1,0:T(8,128)(2,1)S(1)} %pad_maximum_fusion.13), channel_id=1, source_target_pairs={{0,128},{128,0},{1,129},{129,1},{2,130},{130,2},{3,131},{131,3},{4... | collective-permute-start | bytes 344072 | tf_op jit(solution)/shard_map/ppermute | solution.py:23
  211.1 4.8 %collective-permute-done.68 = bf16[112,592]{0,1:T(8,128)(2,1)S(1)} collective-permute-done((bf16[112,592]{0,1:T(8,128)(2,1)S(1)}, bf16[112,592]{0,1:T(8,128)(2,1)S(1)}, u32[]{:S(2)}, u32[]{:S(2)}) %collective-permute-start.68) | collective-permute-done | bytes 132640 | tf_op jit(solution)/shard_map/ppermute | solution.py:23
  218.9 3.2 %collective-permute-start.62 = (bf16[112,592]{0,1:T(8,128)(2,1)S(1)}, bf16[112,592]{0,1:T(8,128)(2,1)S(1)}, u32[]{:S(2)}, u32[]{:S(2)}) collective-permute-start(bf16[112,592]{0,1:T(8,128)(2,1)S(1)} %get-tuple-element.71), channel_id=1, source_target_pairs={{0,96},{32,0},{64,32},{96,64},{1,97},{33,1},{65,33},{97,65},{2,98}... | collective-permute-start | bytes 397832 | tf_op jit(solution)/shard_map/ppermute | solution.py:23
  222.6 3.5 %collective-permute-start.71 = (bf16[224,592]{0,1:T(8,128)(2,1)S(1)}, bf16[224,592]{0,1:T(8,128)(2,1)S(1)}, u32[]{:S(2)}, u32[]{:S(2)}) collective-permute-start(bf16[224,592]{0,1:T(8,128)(2,1)S(1)} %pad_maximum_fusion.6), channel_id=1, source_target_pairs={{0,96},{32,0},{64,32},{96,64},{1,97},{33,1},{65,33},{97,65},{2,98}... | collective-permute-start | bytes 795656 | tf_op jit(solution)/shard_map/ppermute | solution.py:23
  228.8 6.1 %collective-permute-done.69 = bf16[224,592]{0,1:T(8,128)(2,1)S(1)} collective-permute-done((bf16[224,592]{0,1:T(8,128)(2,1)S(1)}, bf16[224,592]{0,1:T(8,128)(2,1)S(1)}, u32[]{:S(2)}, u32[]{:S(2)}) %collective-permute-start.69) | collective-permute-done | bytes 265248 | tf_op jit(solution)/shard_map/ppermute | solution.py:23
  243.9 8.4 %collective-permute-done.72 = bf16[224,592]{0,1:T(8,128)(2,1)S(1)} collective-permute-done((bf16[224,592]{0,1:T(8,128)(2,1)S(1)}, bf16[224,592]{0,1:T(8,128)(2,1)S(1)}, u32[]{:S(2)}, u32[]{:S(2)}) %collective-permute-start.72) | collective-permute-done | bytes 265248 | tf_op jit(solution)/shard_map/ppermute | solution.py:23
  (298 shorter events, 114.4 us)
Async XLA Ops:
  2.2 15.8 %collective-permute-start.1 = (bf16[224,1776]{1,0:T(8,128)(2,1)S(1)}, bf16[224,1776]{1,0:T(8,128)(2,1)}, u32[]{:S(2)}, u32[]{:S(2)}) collective-permute-start(bf16[224,1776]{1,0:T(8,128)(2,1)S(1)} %concatenate.94.refs_0_), channel_id=1, source_target_pairs={{0,16},{16,0},{1,17},{17,1},{2,18},{18,2},{3,19},{19,3},{4,20},{20... | collective-permute-start | bytes 2386952 | tf_op jit(solution)/shard_map/ppermute | solution.py:23
  2.3 20.6 %collective-permute-start.2 = (bf16[224,1776]{1,0:T(8,128)(2,1)S(1)}, bf16[224,1776]{1,0:T(8,128)(2,1)S(1)}, u32[]{:S(2)}, u32[]{:S(2)}) collective-permute-start(bf16[224,1776]{1,0:T(8,128)(2,1)S(1)} %concatenate.94.refs_0_), channel_id=1, source_target_pairs={{0,96},{32,0},{64,32},{96,64},{1,97},{33,1},{65,33},{97,65},{2,98}... | collective-permute-start | bytes 2386952 | tf_op jit(solution)/shard_map/ppermute | solution.py:23
  5.1 21.2 %collective-permute-start.4 = (bf16[224,1776]{1,0:T(8,128)(2,1)S(1)}, bf16[224,1776]{1,0:T(8,128)(2,1)S(1)}, u32[]{:S(2)}, u32[]{:S(2)}) collective-permute-start(bf16[224,1776]{1,0:T(8,128)(2,1)S(1)} %concatenate.94.refs_0_), channel_id=1, source_target_pairs={{0,32},{32,64},{64,96},{96,0},{1,33},{33,65},{65,97},{97,1},{2,34}... | collective-permute-start | bytes 2386952 | tf_op jit(solution)/shard_map/ppermute | solution.py:23
  5.1 42.0 %collective-permute-start = (bf16[224,1776]{1,0:T(8,128)(2,1)S(1)}, bf16[224,1776]{1,0:T(8,128)(2,1)}, u32[]{:S(2)}, u32[]{:S(2)}) collective-permute-start(bf16[224,1776]{1,0:T(8,128)(2,1)S(1)} %concatenate.94.refs_0_), channel_id=1, source_target_pairs={{0,128},{128,0},{1,129},{129,1},{2,130},{130,2},{3,131},{131,3},{4... | collective-permute-start | bytes 2386952 | tf_op jit(solution)/shard_map/ppermute | solution.py:23
  47.9 14.8 %collective-permute-start.22 = (bf16[64,3584]{1,0:T(8,128)(2,1)}, bf16[64,3584]{1,0:T(8,128)(2,1)}, u32[]{:S(2)}, u32[]{:S(2)}) collective-permute-start(bf16[64,3584]{1,0:T(8,128)(2,1)} %pad_maximum_fusion.1), channel_id=1, source_target_pairs={{0,1},{1,2},{2,3},{3,0},{4,5},{5,6},{6,7},{7,4},{8,9},{9,10},{10,1... | collective-permute-start | bytes 1376264 | tf_op jit(solution)/shard_map/ppermute | solution.py:23
  55.7 21.2 %collective-permute-start.14 = (bf16[224,1776]{1,0:T(8,128)(2,1)}, bf16[224,1776]{1,0:T(8,128)(2,1)S(1)}, u32[]{:S(2)}, u32[]{:S(2)}) collective-permute-start(bf16[224,1776]{1,0:T(8,128)(2,1)} %collective-permute-done.refs_10_), channel_id=1, source_target_pairs={{0,32},{32,64},{64,96},{96,0},{1,33},{33,65},{65,97},{97,1},{2,34}... | collective-permute-start | bytes 2386952 | tf_op jit(solution)/shard_map/ppermute | solution.py:23
  56.2 20.7 %collective-permute-start.13 = (bf16[224,1776]{1,0:T(8,128)(2,1)}, bf16[224,1776]{1,0:T(8,128)(2,1)S(1)}, u32[]{:S(2)}, u32[]{:S(2)}) collective-permute-start(bf16[224,1776]{1,0:T(8,128)(2,1)} %collective-permute-done.refs_10_), channel_id=1, source_target_pairs={{0,96},{32,0},{64,32},{96,64},{1,97},{33,1},{65,33},{97,65},{2,98}... | collective-permute-start | bytes 2386952 | tf_op jit(solution)/shard_map/ppermute | solution.py:23
  59.9 20.9 %collective-permute-start.12 = (bf16[32,3712]{1,0:T(8,128)(2,1)S(1)}, bf16[32,3712]{1,0:T(8,128)(2,1)S(1)}, u32[]{:S(2)}, u32[]{:S(2)}) collective-permute-start(bf16[32,3712]{1,0:T(8,128)(2,1)S(1)} %pad_maximum_fusion.7), channel_id=1, source_target_pairs={{0,8},{4,12},{8,0},{12,4},{1,9},{5,13},{9,1},{13,5},{2,10},{6,14},... | collective-permute-start | bytes 712712 | tf_op jit(solution)/shard_map/ppermute | solution.py:38
  80.3 18.6 %collective-permute-start.17 = (bf16[224,1776]{1,0:T(8,128)(2,1)S(1)}, bf16[224,1776]{1,0:T(8,128)(2,1)S(1)}, u32[]{:S(2)}, u32[]{:S(2)}) collective-permute-start(bf16[224,1776]{1,0:T(8,128)(2,1)S(1)} %collective-permute-done.13.refs_11_), channel_id=1, source_target_pairs={{0,16},{16,0},{1,17},{17,1},{2,18},{18,2},{3,19},{19,3},{4,20},{20... | collective-permute-start | bytes 2386952 | tf_op jit(solution)/shard_map/ppermute | solution.py:23
  80.3 21.4 %collective-permute-start.18 = (bf16[224,1776]{1,0:T(8,128)(2,1)S(1)}, bf16[224,1776]{1,0:T(8,128)(2,1)S(1)}, u32[]{:S(2)}, u32[]{:S(2)}) collective-permute-start(bf16[224,1776]{1,0:T(8,128)(2,1)S(1)} %collective-permute-done.14.refs_14_), channel_id=1, source_target_pairs={{0,16},{16,0},{1,17},{17,1},{2,18},{18,2},{3,19},{19,3},{4,20},{20... | collective-permute-start | bytes 2386952 | tf_op jit(solution)/shard_map/ppermute | solution.py:23
  81.7 16.6 %collective-permute-start.15 = (bf16[64,3712]{1,0:T(8,128)(2,1)S(1)}, bf16[64,3712]{1,0:T(8,128)(2,1)S(1)}, u32[]{:S(2)}, u32[]{:S(2)}) collective-permute-start(bf16[64,3712]{1,0:T(8,128)(2,1)S(1)} %pad_maximum_fusion), channel_id=1, source_target_pairs={{0,3},{1,0},{2,1},{3,2},{4,7},{5,4},{6,5},{7,6},{8,11},{9,8},{10,9... | collective-permute-start | bytes 1425416 | tf_op jit(solution)/shard_map/ppermute | solution.py:23
  88.3 24.9 %collective-permute-start.16 = (bf16[64,3712]{1,0:T(8,128)(2,1)S(1)}, bf16[64,3712]{1,0:T(8,128)(2,1)S(1)}, u32[]{:S(2)}, u32[]{:S(2)}) collective-permute-start(bf16[64,3712]{1,0:T(8,128)(2,1)S(1)} %pad_maximum_fusion), channel_id=1, source_target_pairs={{0,1},{1,2},{2,3},{3,0},{4,5},{5,6},{6,7},{7,4},{8,9},{9,10},{10,1... | collective-permute-start | bytes 1425416 | tf_op jit(solution)/shard_map/ppermute | solution.py:23
  98.2 24.0 %collective-permute-start.29 = (bf16[112,1776]{1,0:T(8,128)(2,1)S(1)}, bf16[112,1776]{1,0:T(8,128)(2,1)S(1)}, u32[]{:S(2)}, u32[]{:S(2)}) collective-permute-start(bf16[112,1776]{1,0:T(8,128)(2,1)S(1)} %collective-permute-done.25.refs_12_), channel_id=1, source_target_pairs={{0,16},{16,0},{1,17},{17,1},{2,18},{18,2},{3,19},{19,3},{4,20},{20... | collective-permute-start | bytes 1193480 | tf_op jit(solution)/shard_map/ppermute | solution.py:23
  98.3 23.9 %collective-permute-start.30 = (bf16[112,1776]{1,0:T(8,128)(2,1)S(1)}, bf16[112,1776]{1,0:T(8,128)(2,1)}, u32[]{:S(2)}, u32[]{:S(2)}) collective-permute-start(bf16[112,1776]{1,0:T(8,128)(2,1)S(1)} %collective-permute-done.26.refs_13_), channel_id=1, source_target_pairs={{0,16},{16,0},{1,17},{17,1},{2,18},{18,2},{3,19},{19,3},{4,20},{20... | collective-permute-start | bytes 1193480 | tf_op jit(solution)/shard_map/ppermute | solution.py:23
  98.9 23.1 %collective-permute-start.28 = (bf16[16,3584]{1,0:T(8,128)(2,1)S(1)}, bf16[16,3584]{1,0:T(8,128)(2,1)S(1)}, u32[]{:S(2)}, u32[]{:S(2)}) collective-permute-start(bf16[16,3584]{1,0:T(8,128)(2,1)S(1)} %slice.377), channel_id=1, source_target_pairs={{0,4},{4,0},{8,12},{12,8},{1,5},{5,1},{9,13},{13,9},{2,6},{6,2},{1... | collective-permute-start | bytes 344072 | tf_op jit(solution)/shard_map/ppermute | solution.py:38
  101.7 20.0 %collective-permute-start.20 = (bf16[32,3712]{1,0:T(8,128)(2,1)S(1)}, bf16[32,3712]{1,0:T(8,128)(2,1)S(1)}, u32[]{:S(2)}, u32[]{:S(2)}) collective-permute-start(bf16[32,3712]{1,0:T(8,128)(2,1)S(1)} %slice.268), channel_id=1, source_target_pairs={{0,3},{1,0},{2,1},{3,2},{4,7},{5,4},{6,5},{7,6},{8,11},{9,8},{10,9... | collective-permute-start | bytes 712712 | tf_op jit(solution)/shard_map/ppermute | solution.py:23
  134.6 15.0 %collective-permute-start.37 = (bf16[64,1792]{1,0:T(8,128)(2,1)}, bf16[64,1792]{1,0:T(8,128)(2,1)S(1)}, u32[]{:S(2)}, u32[]{:S(2)}) collective-permute-start(bf16[64,1792]{1,0:T(8,128)(2,1)} %get-tuple-element.51), channel_id=1, source_target_pairs={{0,1},{1,2},{2,3},{3,0},{4,5},{5,6},{6,7},{7,4},{8,9},{9,10},{10,1... | collective-permute-start | bytes 688136 | tf_op jit(solution)/shard_map/ppermute | solution.py:23
  134.7 14.9 %collective-permute-start.38 = (bf16[64,1792]{1,0:T(8,128)(2,1)}, bf16[64,1792]{1,0:T(8,128)(2,1)S(1)}, u32[]{:S(2)}, u32[]{:S(2)}) collective-permute-start(bf16[64,1792]{1,0:T(8,128)(2,1)} %get-tuple-element.52), channel_id=1, source_target_pairs={{0,2},{1,3},{2,0},{3,1},{4,6},{5,7},{6,4},{7,5},{8,10},{9,11},{10,... | collective-permute-start | bytes 688136 | tf_op jit(solution)/shard_map/ppermute | solution.py:23
  137.9 19.0 %collective-permute-start.31 = (bf16[64,1792]{1,0:T(8,128)(2,1)}, bf16[64,1792]{1,0:T(8,128)(2,1)S(1)}, u32[]{:S(2)}, u32[]{:S(2)}) collective-permute-start(bf16[64,1792]{1,0:T(8,128)(2,1)} %get-tuple-element.47), channel_id=1, source_target_pairs={{0,1},{1,2},{2,3},{3,0},{4,5},{5,6},{6,7},{7,4},{8,9},{9,10},{10,1... | collective-permute-start | bytes 688136 | tf_op jit(solution)/shard_map/ppermute | solution.py:23
  138.7 19.4 %collective-permute-start.32 = (bf16[64,1792]{1,0:T(8,128)(2,1)}, bf16[64,1792]{1,0:T(8,128)(2,1)S(1)}, u32[]{:S(2)}, u32[]{:S(2)}) collective-permute-start(bf16[64,1792]{1,0:T(8,128)(2,1)} %get-tuple-element.48), channel_id=1, source_target_pairs={{0,2},{1,3},{2,0},{3,1},{4,6},{5,7},{6,4},{7,5},{8,10},{9,11},{10,... | collective-permute-start | bytes 688136 | tf_op jit(solution)/shard_map/ppermute | solution.py:23
  206.6 31.3 %collective-permute-start.49 = (bf16[8,3584]{1,0:T(8,128)(2,1)S(1)}, bf16[8,3584]{1,0:T(8,128)(2,1)S(1)}, u32[]{:S(2)}, u32[]{:S(2)}) collective-permute-start(bf16[8,3584]{1,0:T(8,128)(2,1)S(1)} %get-tuple-element.89), channel_id=1, source_target_pairs={{0,32},{32,64},{64,96},{96,0},{1,33},{33,65},{65,97},{97,1},{2,34}... | collective-permute-start | bytes 172040 | tf_op jit(solution)/shard_map/ppermute | solution.py:23
  218.8 25.1 %collective-permute-start.61 = (bf16[224,592]{0,1:T(8,128)(2,1)S(1)}, bf16[224,592]{0,1:T(8,128)(2,1)S(1)}, u32[]{:S(2)}, u32[]{:S(2)}) collective-permute-start(bf16[224,592]{0,1:T(8,128)(2,1)S(1)} %pad_maximum_fusion.3), channel_id=1, source_target_pairs={{0,32},{32,64},{64,96},{96,0},{1,33},{33,65},{65,97},{97,1},{2,34}... | collective-permute-start | bytes 795656 | tf_op jit(solution)/shard_map/ppermute | solution.py:23
  226.4 17.5 %collective-permute-start.63 = (bf16[224,592]{0,1:T(8,128)(2,1)S(1)}, bf16[224,592]{0,1:T(8,128)(2,1)S(1)}, u32[]{:S(2)}, u32[]{:S(2)}) collective-permute-start(bf16[224,592]{0,1:T(8,128)(2,1)S(1)} %pad_maximum_fusion.4), channel_id=1, source_target_pairs={{0,96},{32,0},{64,32},{96,64},{1,97},{33,1},{65,33},{97,65},{2,98}... | collective-permute-start | bytes 795656 | tf_op jit(solution)/shard_map/ppermute | solution.py:23
  235.1 17.2 %collective-permute-start.72 = (bf16[224,592]{0,1:T(8,128)(2,1)S(1)}, bf16[224,592]{0,1:T(8,128)(2,1)S(1)}, u32[]{:S(2)}, u32[]{:S(2)}) collective-permute-start(bf16[224,592]{0,1:T(8,128)(2,1)S(1)} %add_convert_fusion.1), channel_id=1, source_target_pairs={{0,128},{128,0},{1,129},{129,1},{2,130},{130,2},{3,131},{131,3},{4... | collective-permute-start | bytes 795656 | tf_op jit(solution)/shard_map/ppermute | solution.py:23
  (77 other events, 745.8 us)
